TPU v7x, 512 devices: a whole 4x4x16 slice. The times are simulated.
512 devices in a mesh: dom: 128 (over z, y, x_lo), edge: 4 (over x_hi, core).
Axes of the slice: x: 4 (x_hi: 2, x_lo: 2; x = x_hi * 2 + x_lo), y: 4, z: 16, core: 2. Of those that a mesh axis runs over, the one named last changes fastest.
Arguments:
- embeddings: float32 [65536, 400], P(('dom', 'edge')), may hold values from -1.2 to 1.2
- adagrad_state: float32 [65536], P(('dom', 'edge')), may hold values from 0.01 to 1
- relations: bfloat16 [256, 400], replicated, may hold values from -4 to 4
- endpoints: int32 [2, 2, 128, 2048], P(None, None, 'dom', 'edge'), may hold values from 0 to 511
- relation_ids: int32 [2, 128, 2048], P(None, 'dom', 'edge'), may hold values from 0 to 255
- negatives: int32 [2, 2, 128, 8, 256], P(None, None, 'dom', 'edge'), may hold values from 0 to 511
- edge_counts: int32 [2, 128, 4], P(None, 'dom', 'edge'), may hold values from 1 to 512, as said below
- plan: int32 [2], replicated, may hold values from 1 to 127, as said below
Outputs:
- new_embeddings: float32 [65536, 400], P(('dom', 'edge'))
- new_state: float32 [65536], P(('dom', 'edge'))
Inputs may be any that keep to these rules, and one draw needn't show every extreme that they name: `edge_counts`: in every round some edge group has all 512 slots live; live slots come first. `plan`: consecutive rounds have different patterns; some round has the pattern 128 - 1.
All inputs are finite; a program needn't handle non-finite values.
Results may differ from a plain program's by a relative error of at most 0.01.
Values may be sent and summed in bfloat16 or wider, within the bound.
A program may use at most 64 MiB of HBM per device.

v0:
```python
import functools

import jax
import jax.numpy as jnp
from jax import lax
from jax.experimental import pallas as pl
from jax.experimental.pallas import tpu as pltpu
from jax.sharding import PartitionSpec as P

MESH = pl.DeviceIdType.MESH
learning_rate = 0.2
LANES = 128
LOW_BITS = 3
IDX_ROWS = 16


def xor(value, mask):
    out = value
    for bit in range(mask.bit_length()):
        if mask >> bit & 1:
            out = out + (1 << bit) * (1 - 2 * (value // (1 << bit) % 2))
    return out


def columns(index):
    return pl.ds(pl.multiple_of(index * LANES, LANES), LANES)


def greet(devices):
    barrier = pltpu.get_barrier_semaphore()
    for device in devices:
        pl.semaphore_signal(barrier, inc=1, device_id=device, device_id_type=MESH)


def greeted(count):
    pl.semaphore_wait(pltpu.get_barrier_semaphore(), count)


def far_kernel(mask, mine, idx, own_full, other, other_idx, send, recv, local):
    dom, edge = lax.axis_index("dom"), lax.axis_index("edge")
    mates = [(dom, (edge + k) % 4) for k in range(1, 4)]
    across = (xor(dom, mask << LOW_BITS), edge)
    greet(mates + ([across] if mask else []))
    greeted(4 if mask else 3)
    copies = []
    if mask:
        for at, (src, dst) in enumerate(((mine, other), (idx, other_idx))):
            copies.append(
                pltpu.make_async_remote_copy(
                    src, dst, send.at[at], recv.at[at], device_id=across, device_id_type=MESH
                )
            )
    for k, mate in enumerate(mates):
        copies.append(
            pltpu.make_async_remote_copy(
                mine,
                own_full.at[:, columns(edge)],
                send.at[2 + k],
                recv.at[2 + k],
                device_id=mate,
                device_id_type=MESH,
            )
        )
    kept = pltpu.make_async_copy(mine, own_full.at[:, columns(edge)], local.at[0])
    for copy in copies:
        copy.start()
    kept.start()
    if not mask:
        other[...] = mine[...]
        other_idx[...] = idx[...]
    kept.wait()
    for copy in copies:
        copy.wait()


def near_kernel(mask, shard, idx, full, full_idx, send, recv, local):
    dom, edge = lax.axis_index("dom"), lax.axis_index("edge")
    chip, core = edge // 2, edge % 2
    partner = xor(dom, mask)
    sibling = (dom, chip * 2 + (1 - core))
    other_chip = (dom, (1 - chip) * 2 + core)
    targets = [(partner, edge), (partner, (1 - chip) * 2 + core)]
    if mask:
        greet([sibling] + targets)
        greeted(3)
    else:
        greet([sibling, other_chip])
        greeted(2)
    here, there = columns(edge), columns((1 - chip) * 2 + core)
    straight = crossed = moved = None
    crossed = pltpu.make_async_remote_copy(
        shard, full.at[:, here], send.at[1], recv.at[1], device_id=targets[1], device_id_type=MESH
    )
    crossed.start()
    if mask:
        straight = pltpu.make_async_remote_copy(
            shard, full.at[:, here], send.at[0], recv.at[0], device_id=targets[0], device_id_type=MESH
        )
        moved = pltpu.make_async_remote_copy(
            idx, full_idx, send.at[2], recv.at[2], device_id=targets[0], device_id_type=MESH
        )
        straight.start()
        moved.start()
    else:
        kept = pltpu.make_async_copy(shard, full.at[:, here], local.at[0])
        kept.start()
        full_idx[...] = idx[...]
        kept.wait()
    if mask:
        straight.wait_recv()
    first = pltpu.make_async_remote_copy(
        full.at[:, here],
        full.at[:, here],
        send.at[3],
        recv.at[3],
        device_id=sibling,
        device_id_type=MESH,
    )
    first.start()
    crossed.wait_recv()
    second = pltpu.make_async_remote_copy(
        full.at[:, there],
        full.at[:, there],
        send.at[4],
        recv.at[4],
        device_id=sibling,
        device_id_type=MESH,
    )
    second.start()
    crossed.wait_send()
    if mask:
        straight.wait_send()
        moved.wait()
    first.wait()
    second.wait()


def across_rows(left, right):
    return lax.dot_general(left, right, (((1,), (1,)), ((), ())), preferred_element_type=jnp.float32)


def product(left, right):
    return jnp.dot(left, right, preferred_element_type=jnp.float32)


def halves(values):
    half = values.shape[0] // 2
    return values[:half], values[half:]


def ones_where(condition):
    return jnp.where(condition, 1.0, 0.0)


def round_kernel(
    own, other, idx, other_idx, relations, table, state,
    table_out, state_out, shard_out,
    own_rows, other_rows, total, parts, arrived, send, recv,
):
    dom, edge = lax.axis_index("dom"), lax.axis_index("edge")
    mates = [(dom, (edge + k) % 4) for k in range(1, 4)]
    greet(mates)
    rows = own.shape[1]
    width = own.shape[0]
    block = 2 * LANES
    own_rows[...] = own[...].T
    other_rows[...] = other[...].T
    total[...] = jnp.zeros_like(total)

    def packed(group, base, at):
        def row(ref, i):
            return ref[pl.ds(base + at + i, 1), :]

        both = [
            jnp.where(group == 0, row(idx, i), row(other_idx, i)) for i in range(2)
        ]
        both = jnp.concatenate(both, axis=1)
        return both & 65535, both >> 16

    def step(b, carry):
        group, at = b // 2, b % 2 * 2
        own_ids, other_ids = packed(group, 0, at)
        rel_ids, count = packed(group, 4, at)
        own_neg, other_neg = packed(group, 8, at)
        row_of = lax.broadcasted_iota(jnp.int32, (rows, block), 0)
        slot = lax.broadcasted_iota(jnp.int32, (1, block), 1) + b % 2 * block
        live = ones_where(slot < count)
        sign = (1 - 2 * group).astype(jnp.float32)
        pick_own = ones_where(row_of == own_ids).astype(jnp.bfloat16)
        pick_other = ones_where(row_of == other_ids).astype(jnp.bfloat16)
        rel_row = lax.broadcasted_iota(jnp.int32, (relations.shape[1], block), 0)
        pick_rel = ones_where(rel_row == rel_ids).astype(jnp.bfloat16)

        def counts(ids):
            hits = ones_where(row_of == ids)
            hits = (hits[:, :LANES] + hits[:, LANES:]).astype(jnp.bfloat16)
            return product(hits, jnp.full((LANES, block), 1.0, jnp.bfloat16))

        mine = product(own[...], pick_own)
        theirs = product(other[...], pick_other)
        rel_re, rel_im = halves(product(relations[...], pick_rel))
        rel_im = rel_im * sign
        m_re, m_im = halves(mine)
        t_re, t_im = halves(theirs)
        u = jnp.concatenate([m_re * rel_re - m_im * rel_im, m_re * rel_im + m_im * rel_re], axis=0)
        v = jnp.concatenate([rel_re * t_re + rel_im * t_im, rel_re * t_im - rel_im * t_re], axis=0)
        u_low = u.astype(jnp.bfloat16)
        v_low = v.astype(jnp.bfloat16)
        positive = jnp.sum(u_low.astype(jnp.float32) * theirs, axis=0, keepdims=True)
        weight_pos = -jax.nn.sigmoid(-positive) * live
        share = live * (0.5 / rows)

        def weights(scores, ids):
            return ((1.0 + jnp.tanh(0.5 * scores)) * (counts(ids) * share)).astype(jnp.bfloat16)

        w_other = weights(product(other_rows[...], u_low), other_neg)
        w_own = weights(product(own_rows[...], v_low), own_neg)
        grad = weight_pos * theirs + product(other[...], w_other)
        g_re, g_im = halves(grad)
        grad = jnp.concatenate(
            [g_re * rel_re + g_im * rel_im, g_im * rel_re - g_re * rel_im], axis=0
        ).astype(jnp.bfloat16)
        total[...] += across_rows(grad, pick_own) + across_rows(v_low, w_own)
        return carry

    lax.fori_loop(0, 4, step, 0)
    for e in range(4):
        parts[e] = total[:, e * LANES : (e + 1) * LANES].astype(jnp.bfloat16)
    greeted(3)
    copies = [
        pltpu.make_async_remote_copy(
            parts.at[(edge + k) % 4],
            arrived.at[k - 1],
            send.at[k - 1],
            recv.at[k - 1],
            device_id=mates[k - 1],
            device_id_type=MESH,
        )
        for k in range(1, 4)
    ]
    for copy in copies:
        copy.start()
    for copy in copies:
        copy.wait()
    grad = parts[edge].astype(jnp.float32)
    for k in range(3):
        grad = grad + arrived[k].astype(jnp.float32)
    new_state = state[...] + jnp.sum(grad * grad, axis=0, keepdims=True) * (1.0 / width)
    new_table = table[...] - learning_rate * grad / jnp.sqrt(new_state)
    state_out[...] = new_state
    table_out[...] = new_table
    shard_out[...] = new_table.astype(jnp.bfloat16)


VMEM = pl.BlockSpec(memory_space=pltpu.VMEM)
DMA = pltpu.SemaphoreType.DMA
LIMIT = 24 * 2**20


def far(mask, shard, idx):
    width = shard.shape[0]
    return pl.pallas_call(
        functools.partial(far_kernel, mask),
        out_shape=(
            jax.ShapeDtypeStruct((width, 4 * LANES), jnp.bfloat16),
            jax.ShapeDtypeStruct(shard.shape, jnp.bfloat16),
            jax.ShapeDtypeStruct(idx.shape, jnp.int32),
        ),
        in_specs=[VMEM] * 2,
        out_specs=(VMEM,) * 3,
        scratch_shapes=[DMA((5,)), DMA((5,)), DMA((1,))],
        compiler_params=pltpu.CompilerParams(
            collective_id=mask, has_side_effects=True, vmem_limit_bytes=LIMIT
        ),
        name=f"far_{mask}",
    )(shard, idx)


def near(mask, shard, idx):
    width = shard.shape[0]
    return pl.pallas_call(
        functools.partial(near_kernel, mask),
        out_shape=(
            jax.ShapeDtypeStruct((width, 4 * LANES), jnp.bfloat16),
            jax.ShapeDtypeStruct(idx.shape, jnp.int32),
        ),
        in_specs=[VMEM] * 2,
        out_specs=(VMEM,) * 2,
        scratch_shapes=[DMA((5,)), DMA((5,)), DMA((1,))],
        compiler_params=pltpu.CompilerParams(
            collective_id=16 + mask, has_side_effects=True, vmem_limit_bytes=LIMIT
        ),
        name=f"near_{mask}",
    )(shard, idx)


def one_round(own, other, idx, other_idx, relations, table, state):
    width, rows = own.shape
    return pl.pallas_call(
        round_kernel,
        out_shape=(
            jax.ShapeDtypeStruct(table.shape, jnp.float32),
            jax.ShapeDtypeStruct(state.shape, jnp.float32),
            jax.ShapeDtypeStruct(table.shape, jnp.bfloat16),
        ),
        in_specs=[VMEM] * 7,
        out_specs=(VMEM,) * 3,
        scratch_shapes=[
            pltpu.VMEM((rows, width), jnp.bfloat16),
            pltpu.VMEM((rows, width), jnp.bfloat16),
            pltpu.VMEM((width, rows), jnp.float32),
            pltpu.VMEM((4, width, LANES), jnp.bfloat16),
            pltpu.VMEM((3, width, LANES), jnp.bfloat16),
            DMA((3,)),
            DMA((3,)),
        ],
        compiler_params=pltpu.CompilerParams(
            collective_id=24, has_side_effects=True, vmem_limit_bytes=LIMIT
        ),
        name="one_round",
    )(own, other, idx, other_idx, relations, table, state)


def packed_edges(own_ids, other_ids, rel_ids, own_neg, other_neg, count):
    rows = jnp.stack(
        [
            own_ids + other_ids * 65536,
            rel_ids + count * 65536,
            own_neg + other_neg * 65536,
        ]
    ).reshape(-1, LANES)
    return jnp.pad(rows, ((0, IDX_ROWS - rows.shape[0]), (0, 0)))


def on_device(
    embeddings, adagrad_state, relations, endpoints, relation_ids, negatives, edge_counts, plan
):
    table = embeddings.T
    shard = table.astype(jnp.bfloat16)
    state = adagrad_state[None, :]
    relations = relations.T
    for r in range(plan.shape[0]):
        ends = (endpoints[r, 0, 0], endpoints[r, 1, 0])
        negs = (negatives[r, 0, 0].reshape(-1), negatives[r, 1, 0].reshape(-1))
        rel_ids, count = relation_ids[r, 0], edge_counts[r, 0]
        here = packed_edges(ends[0], ends[1], rel_ids, negs[0], negs[1], count)
        away = packed_edges(ends[1], ends[0], rel_ids, negs[1], negs[0], count)
        high, low = plan[r] >> LOW_BITS, plan[r] & (2**LOW_BITS - 1)
        own, other, idx = lax.switch(
            high, [functools.partial(far, mask) for mask in range(16)], shard, away
        )
        other, idx = lax.switch(
            low, [functools.partial(near, mask) for mask in range(8)], other, idx
        )
        table, state, shard = one_round(own, other, here, idx, relations, table, state)
    return table.T, state[0]


def solution(mesh):
    in_specs = (
        P(("dom", "edge"), None),
        P(("dom", "edge")),
        P(),
        P(None, None, "dom", "edge"),
        P(None, "dom", "edge"),
        P(None, None, "dom", "edge", None),
        P(None, "dom", "edge"),
        P(),
    )
    out_specs = (P(("dom", "edge"), None), P(("dom", "edge")))
    return jax.shard_map(
        on_device, mesh=mesh, in_specs=in_specs, out_specs=out_specs, check_vma=False
    )
```

profile of v0, /device:TPU:1, one launch (start us, length us, event | category | flops | bytes accessed | tf_op | source)
XLA Modules:
  0.0 107.6 jit_solution(15694928366885449872)
XLA Ops:
  0.6 0.0 copy-start.1
  0.6 1.3 %fusion.6 = (s32[1,1,1]{0,2,1:T(1,128)}, s32[1,1,1]{0,2,1:T(1,128)}) fusion(s32[2,1,1]{0,2,1:T(1,128)} %param.62), kind=kLoop, calls=%fused_computation.27 | loop fusion | bytes 16 | tf_op jit(solution)/shard_map/slice | solution.py:345
  3.3 1.3 %fusion.7 = (s32[1]{0:T(128)}, s32[1]{0:T(128)}) fusion(s32[2]{0:T(128)} %param.63), kind=kLoop, calls=%fused_computation.28 | loop fusion | bytes 16 | tf_op jit(solution)/shard_map/slice | solution.py:348
  7.2 0.7 add_bitcast_fusion
  7.9 0.7 bitcast_add_fusion
  8.6 0.7 slice_bitcast_fusion
  9.6 0.0 copy-done.1
  9.6 23.3 %conditional.4 = ((bf16[400,512]{1,0:T(8,128)(2,1)S(1)}, bf16[400,128]{1,0:T(8,128)(2,1)S(1)}, s32[16,128]{1,0:T(8,128)S(1)})) conditional(s32[]{:T(128)} %bitcast.1, (bf16[400,128]{1,0:T(8,128)(2,1)S(1)}, s32[16,128]{1,0:T(8,128)S(1)}) %tuple.152, (bf16[400,128]{1,0:T(8,128)(2,1)S(1)}, ...), branch_computations={%region_0.1_spmd, %region_1.2_spmd, %region_2.3_spmd, %region_3.4_... | conditional | bytes 8 | solution.py:349
  9.6 23.3 %far_8.2 = (bf16[400,512]{1,0:T(8,128)(2,1)S(1)}, bf16[400,128]{1,0:T(8,128)(2,1)S(1)}, s32[16,128]{1,0:T(8,128)S(1)}) custom-call(bf16[400,128]{1,0:T(8,128)(2,1)S(1)} %get-tuple-element.208.mine, s32[16,128]{1,0:T(8,128)S(1)} %get-tuple-element.209.idx), custom_call_target="tpu_custom_call" | custom-call | tf_op jit(solution)/shard_map/cond/branch_8_fun/far_8/pallas_call | solution.py:262
  32.9 0.0 copy-start
  32.9 10.4 %conditional.5 = ((bf16[400,512]{1,0:T(8,128)(2,1)S(1)}, s32[16,128]{1,0:T(8,128)S(1)})) conditional(s32[]{:T(128)} %bitcast.7, (bf16[400,128]{1,0:T(8,128)(2,1)S(1)}, s32[16,128]{1,0:T(8,128)S(1)}) %tuple.153, (bf16[400,128]{1,0:T(8,128)(2,1)S(1)}, s32[16,128]{1,0:T(8,128)S(1)}) %tuple.153, ...), branch_computations={%region_16.17_spmd, %region_17.18_spmd, %region_18.19_spmd, %regio... | conditional | bytes 8 | solution.py:352
  33.0 10.3 %near_3.2 = (bf16[400,512]{1,0:T(8,128)(2,1)S(1)}, s32[16,128]{1,0:T(8,128)S(1)}) custom-call(bf16[400,128]{1,0:T(8,128)(2,1)S(1)} %get-tuple-element.230.shard, s32[16,128]{1,0:T(8,128)S(1)} %get-tuple-element.231.idx), custom_call_target="tpu_custom_call" | custom-call | tf_op jit(solution)/shard_map/cond/branch_3_fun/near_3/pallas_call | solution.py:281
  43.3 0.0 copy-start.2
  43.3 0.0 copy-done
  43.3 0.6 copy-done.2
  44.0 15.5 %one_round.2 = (f32[400,128]{1,0:T(8,128)S(1)}, f32[1,128]{1,0:T(1,128)S(1)}, bf16[400,128]{1,0:T(8,128)(2,1)S(1)}) custom-call(bf16[400,512]{1,0:T(8,128)(2,1)S(1)} %get-tuple-element.305.own, bf16[400,512]{1,0:T(8,128)(2,1)S(1)} %get-tuple-element.308.other, s32[16,128]{1,0:T(8,128)S(1)} %pad.14.idx, s32[16,128]{1,0:T(8,128)S(1)} %get-tuple-element.309.other_idx, ...), custom_call_target="tpu_custom_call" | custom-call | tf_op jit(solution)/shard_map/one_round/pallas_call | solution.py:299
  59.5 16.4 %conditional.6 = ((bf16[400,512]{1,0:T(8,128)(2,1)S(1)}, bf16[400,128]{1,0:T(8,128)(2,1)S(1)}, s32[16,128]{1,0:T(8,128)S(1)})) conditional(s32[]{:T(128)} %bitcast, (bf16[400,128]{1,0:T(8,128)(2,1)S(1)}, s32[16,128]{1,0:T(8,128)S(1)}) %tuple.154, (bf16[400,128]{1,0:T(8,128)(2,1)S(1)}, ...), branch_computations={%region_24.25_spmd, %region_25.26_spmd, %region_26.27_spmd, %regio... | conditional | bytes 8 | solution.py:349
  59.6 16.3 %far_15.3 = (bf16[400,512]{1,0:T(8,128)(2,1)S(1)}, bf16[400,128]{1,0:T(8,128)(2,1)S(1)}, s32[16,128]{1,0:T(8,128)S(1)}) custom-call(bf16[400,128]{1,0:T(8,128)(2,1)S(1)} %get-tuple-element.270.mine, s32[16,128]{1,0:T(8,128)S(1)} %get-tuple-element.271.idx), custom_call_target="tpu_custom_call" | custom-call | tf_op jit(solution)/shard_map/cond/branch_15_fun/far_15/pallas_call | solution.py:262
  75.9 14.4 %conditional.7 = ((bf16[400,512]{1,0:T(8,128)(2,1)S(1)}, s32[16,128]{1,0:T(8,128)S(1)})) conditional(s32[]{:T(128)} %bitcast.14, (bf16[400,128]{1,0:T(8,128)(2,1)S(1)}, s32[16,128]{1,0:T(8,128)S(1)}) %tuple.155, (bf16[400,128]{1,0:T(8,128)(2,1)S(1)}, s32[16,128]{1,0:T(8,128)S(1)}) %tuple.155, ...), branch_computations={%region_40.41_spmd, %region_41.42_spmd, %region_42.43_spmd, %regio... | conditional | bytes 8 | solution.py:352
  76.0 14.3 %near_7.3 = (bf16[400,512]{1,0:T(8,128)(2,1)S(1)}, s32[16,128]{1,0:T(8,128)S(1)}) custom-call(bf16[400,128]{1,0:T(8,128)(2,1)S(1)} %get-tuple-element.286.shard, s32[16,128]{1,0:T(8,128)S(1)} %get-tuple-element.287.idx), custom_call_target="tpu_custom_call" | custom-call | tf_op jit(solution)/shard_map/cond/branch_7_fun/near_7/pallas_call | solution.py:281
  90.3 16.1 %one_round.3 = (f32[400,128]{1,0:T(8,128)S(1)}, f32[1,128]{1,0:T(1,128)S(1)}, bf16[400,128]{1,0:T(8,128)(2,1)}) custom-call(bf16[400,512]{1,0:T(8,128)(2,1)S(1)} %get-tuple-element.311.own, bf16[400,512]{1,0:T(8,128)(2,1)S(1)} %get-tuple-element.314.other, s32[16,128]{1,0:T(8,128)S(1)} %pad.16.idx, s32[16,128]{1,0:T(8,128)S(1)} %get-tuple-element.315.other_idx, ...), custom_call_target="tpu_custom_call" | custom-call | tf_op jit(solution)/shard_map/one_round/pallas_call | solution.py:299
  106.4 0.7 copy.144
  107.1 0.5 copy.145
  (16 shorter events, 0.1 us)
Async XLA Ops:
  0.6 8.9 %copy-start.1 = (f32[128,400]{0,1:T(8,128)S(1)}, f32[128,400]{0,1:T(8,128)}, u32[]{:S(2)}) copy-start(f32[128,400]{0,1:T(8,128)} %param.56) | copy-start | bytes 614404
  32.9 10.4 %copy-start = (bf16[256,400]{0,1:T(8,128)(2,1)S(1)}, bf16[256,400]{0,1:T(8,128)(2,1)}, u32[]{:S(2)}) copy-start(bf16[256,400]{0,1:T(8,128)(2,1)} %param.58) | copy-start | bytes 614404
  43.3 0.7 copy-start.2
where the time goes:
time: 108 us
  Pallas kernels  95.9 us (89%)
  local copies, waits for them, and re-layouts  5.29 us (5%)
  between operations  4.71 us (4%)
  other arithmetic  1.5 us (1%)
    pallas_call x2, Pallas kernels, far(): pl.pallas_call(functools.partial(far_kernel, mask), out_shape=(jax.ShapeD...  39.6 us
    pallas_call x2, Pallas kernels, one_round(): pl.pallas_call(round_kernel, out_shape=(jax.ShapeDtypeStruct(table.shape,...  31.6 us
    pallas_call x2, Pallas kernels, near(): pl.pallas_call(functools.partial(near_kernel, mask), out_shape=(jax.Shape...  24.7 us
    unnamed x13, local copies, waits for them, and re-layouts  2.6 us

commit v1 on v0

v1 whole, which is shorter than its diff:
```python
import functools

import jax
import jax.numpy as jnp
from jax import lax
from jax.experimental import pallas as pl
from jax.experimental.pallas import tpu as pltpu
from jax.sharding import PartitionSpec as P

MESH = pl.DeviceIdType.MESH
learning_rate = 0.2
LANES = 128
LOW_BITS = 3
BLOCK = 256


def xor(value, mask):
    out = value
    for bit in range(mask.bit_length()):
        if mask >> bit & 1:
            out = out + (1 << bit) * (1 - 2 * (value // (1 << bit) % 2))
    return out


def columns(index):
    return pl.ds(pl.multiple_of(index * LANES, LANES), LANES)


def greet(devices):
    barrier = pltpu.get_barrier_semaphore()
    for device in devices:
        pl.semaphore_signal(barrier, inc=1, device_id=device, device_id_type=MESH)


def greeted(count):
    pl.semaphore_wait(pltpu.get_barrier_semaphore(), count)


def far_kernel(mask, mine, idx, own_full, other, other_idx, send, recv, local):
    dom, edge = lax.axis_index("dom"), lax.axis_index("edge")
    mates = [(dom, (edge + k) % 4) for k in range(1, 4)]
    across = (xor(dom, mask << LOW_BITS), edge)
    greet(mates + ([across] if mask else []))
    kept = pltpu.make_async_copy(mine, own_full.at[:, columns(edge)], local.at[0])
    kept.start()
    greeted(4 if mask else 3)
    copies = []
    if mask:
        for at, (src, dst) in enumerate(((mine, other), (idx, other_idx))):
            copies.append(
                pltpu.make_async_remote_copy(
                    src, dst, send.at[at], recv.at[at], device_id=across, device_id_type=MESH
                )
            )
    for k, mate in enumerate(mates):
        copies.append(
            pltpu.make_async_remote_copy(
                mine,
                own_full.at[:, columns(edge)],
                send.at[2 + k],
                recv.at[2 + k],
                device_id=mate,
                device_id_type=MESH,
            )
        )
    for copy in copies:
        copy.start()
    if not mask:
        other[...] = mine[...]
        other_idx[...] = idx[...]
    kept.wait()
    for copy in copies:
        copy.wait()


def pack_kernel(table, ends, rels, negs, counts, shard, *packed):
    shard[...] = table[...].astype(jnp.bfloat16)
    for r in range(2):
        here, away = packed[2 * r : 2 * r + 2]
        left, right = ends[r, 0], ends[r, 1]
        rel = rels[r] + counts[r] * 65536
        there, back = left + right * 65536, right + left * 65536
        for half in range(2):
            at = slice(half * BLOCK, (half + 1) * BLOCK)
            left_neg = negs[r, 0, 0, half : half + 1]
            right_neg = negs[r, 1, 0, half : half + 1]
            for out, ids, neg in (
                (here, there, left_neg + right_neg * 65536),
                (away, back, right_neg + left_neg * 65536),
            ):
                out[half : half + 1] = ids[:, at]
                out[2 + half : 3 + half] = rel[:, at]
                out[4 + half : 5 + half] = neg
        for out in (here, away):
            out[6:8] = jnp.zeros((2, BLOCK), jnp.int32)


def across_rows(left, right):
    return lax.dot_general(left, right, (((1,), (1,)), ((), ())), preferred_element_type=jnp.float32)


def product(left, right):
    return jnp.dot(left, right, preferred_element_type=jnp.float32)


def halves(values):
    half = values.shape[0] // 2
    return values[:half], values[half:]


def ones_where(condition):
    return jnp.where(condition, 1.0, 0.0)


CHUNKS = ((0, 208), (208, 192))


def near_kernel(mask, shard, idx, full, full_idx, send, recv, local):
    dom, edge = lax.axis_index("dom"), lax.axis_index("edge")
    chip, core = edge // 2, edge % 2
    partner = xor(dom, mask)
    other = (1 - chip) * 2 + core
    straight, crossed, sibling = (partner, edge), (partner, other), (dom, chip * 2 + (1 - core))
    greet([crossed, sibling] + ([straight] if mask else []))
    if not mask:
        kept = pltpu.make_async_copy(shard, full.at[:, columns(edge)], local.at[0])
        kept.start()
        full_idx[...] = idx[...]
    greeted(3 if mask else 2)

    def chunk(ref, piece, column):
        return ref.at[pl.ds(*CHUNKS[piece]), columns(column)]

    def moved(src, dst, at, device):
        return pltpu.make_async_remote_copy(
            src, dst, send.at[at], recv.at[at], device_id=device, device_id_type=MESH
        )

    away = [
        [
            moved(shard.at[pl.ds(*CHUNKS[piece]), :], chunk(full, piece, edge), 2 * piece + k, device)
            for k, device in enumerate((crossed, straight) if mask else (crossed,))
        ]
        for piece in range(2)
    ]
    ids = [moved(idx, full_idx, 8, straight)] if mask else []
    for copy in away[0] + ids + away[1]:
        copy.start()
    if not mask:
        kept.wait()
    forwards = []
    for piece in range(2):
        for k, copy in enumerate(away[piece]):
            copy.wait_recv()
            here = chunk(full, piece, edge if k else other)
            forwards.append(moved(here, here, 4 + 2 * piece + k, sibling))
            forwards[-1].start()
        if not mask:
            here = chunk(full, piece, edge)
            forwards.append(moved(here, here, 5 + 2 * piece, sibling))
            forwards[-1].start()
    for copy in away[0] + away[1]:
        copy.wait_send()
    for copy in ids + forwards:
        copy.wait()


def round_kernel(
    other, other_idx, own, here_idx, relations, table, state,
    table_out, state_out, shard_out,
    own_rows, other_rows, rel_kept, factors, grads, pick_own, weights_own, parts, arrived,
    send, recv,
):
    dom, edge = lax.axis_index("dom"), lax.axis_index("edge")
    chip, core = edge // 2, edge % 2
    sibling = (dom, chip * 2 + (1 - core))
    mates = [
        (dom, (1 - chip) * 2 + core),
        (dom, (1 - chip) * 2 + (1 - core)),
        sibling,
    ]
    greet(mates)
    width, rows = own.shape

    def ids_of(b, kind):
        ref = other_idx if b // 2 else here_idx
        return ref[2 * kind + b % 2 : 2 * kind + b % 2 + 1]

    def picked(ids, count):
        row_of = lax.broadcasted_iota(jnp.int32, (count, BLOCK), 0)
        return ones_where(row_of == ids).astype(jnp.bfloat16)

    def own_side(b):
        at = slice(b * BLOCK, (b + 1) * BLOCK)
        chosen = picked(ids_of(b, 0) & 65535, rows)
        pick_own[:, at] = chosen
        m_re, m_im = halves(product(own[...], chosen))
        pick_rel = picked(ids_of(b, 1) & 65535, relations.shape[1])
        rel_re, rel_im = halves(product(relations[...], pick_rel))
        if b // 2:
            rel_im = -rel_im
        rel_kept[:, at] = jnp.concatenate([rel_re, rel_im], axis=0).astype(jnp.bfloat16)
        grads[:, at] = jnp.concatenate(
            [m_re * rel_re - m_im * rel_im, m_re * rel_im + m_im * rel_re], axis=0
        ).astype(jnp.bfloat16)

    def weights(scores, ids, share):
        hits = picked(ids, rows)
        hits = product(hits[:, :LANES] + hits[:, LANES:], jnp.full((LANES, LANES), 1.0, jnp.bfloat16))
        hits = jnp.concatenate([hits, hits], axis=1) * share
        return ((1.0 + jnp.tanh(0.5 * scores)) * hits).astype(jnp.bfloat16)

    def both_sides(b):
        at = slice(b * BLOCK, (b + 1) * BLOCK)
        slot = lax.broadcasted_iota(jnp.int32, (1, BLOCK), 1) + b % 2 * BLOCK
        live = ones_where(slot < ids_of(b, 1) >> 16)
        share = live * (0.5 / rows)
        theirs = product(other[...], picked(ids_of(b, 0) >> 16, rows))
        rel_re, rel_im = halves(rel_kept[:, at].astype(jnp.float32))
        t_re, t_im = halves(theirs)
        u_low = grads[:, at]
        v_low = jnp.concatenate(
            [rel_re * t_re + rel_im * t_im, rel_re * t_im - rel_im * t_re], axis=0
        ).astype(jnp.bfloat16)
        factors[:, at] = v_low
        positive = jnp.sum(u_low.astype(jnp.float32) * theirs, axis=0, keepdims=True)
        weight_pos = -jax.nn.sigmoid(-positive) * live
        negs = ids_of(b, 2)
        w_other = weights(product(other_rows[...], u_low), negs >> 16, share)
        weights_own[:, at] = weights(product(own_rows[...], v_low), negs & 65535, share)
        grad = weight_pos * theirs + product(other[...], w_other)
        g_re, g_im = halves(grad)
        grads[:, at] = jnp.concatenate(
            [g_re * rel_re + g_im * rel_im, g_im * rel_re - g_re * rel_im], axis=0
        ).astype(jnp.bfloat16)

    own_rows[...] = own[...].T
    other_rows[...] = other[...].T
    for b in range(4):
        own_side(b)
        both_sides(b)

    def partial(which):
        at = pl.ds(pl.multiple_of(which * BLOCK, BLOCK), BLOCK)
        total = across_rows(grads[...], pick_own[at, :]) + across_rows(
            factors[...], weights_own[at, :]
        )
        total = total.astype(jnp.bfloat16)
        parts[2 * which] = total[:, :LANES]
        parts[2 * which + 1] = total[:, LANES:]

    gifts = [
        pltpu.make_async_remote_copy(
            parts.at[mate[1]],
            arrived.at[k],
            send.at[k],
            recv.at[k],
            device_id=mate,
            device_id_type=MESH,
        )
        for k, mate in enumerate(mates)
    ]
    partial(1 - chip)
    greeted(3)
    gifts[0].start()
    gifts[1].start()
    partial(chip)
    gifts[2].start()
    grad = parts[edge].astype(jnp.float32)
    for k in (2, 0, 1):
        gifts[k].wait_recv()
        grad = grad + arrived[k].astype(jnp.float32)
    new_state = state[...] + jnp.sum(grad * grad, axis=0, keepdims=True) * (1.0 / width)
    new_table = table[...] - learning_rate * grad / jnp.sqrt(new_state)
    shard_out[...] = new_table.astype(jnp.bfloat16)
    state_out[...] = new_state
    table_out[...] = new_table
    for copy in gifts:
        copy.wait_send()


VMEM = pl.BlockSpec(memory_space=pltpu.VMEM)
DMA = pltpu.SemaphoreType.DMA
LIMIT = 24 * 2**20


def shape(*dims, dtype=jnp.bfloat16):
    return jax.ShapeDtypeStruct(dims, dtype)


def like(array, dtype=None):
    return jax.ShapeDtypeStruct(array.shape, dtype or array.dtype)


def params(collective_id):
    return pltpu.CompilerParams(
        collective_id=collective_id, has_side_effects=True, vmem_limit_bytes=LIMIT
    )


def pack(table, ends, rels, negs, counts):
    idx = shape(8, BLOCK, dtype=jnp.int32)
    return pl.pallas_call(
        pack_kernel,
        out_shape=(like(table, jnp.bfloat16),) + (idx,) * 4,
        in_specs=[VMEM] * 5,
        out_specs=(VMEM,) * 5,
        compiler_params=pltpu.CompilerParams(vmem_limit_bytes=LIMIT),
        name="pack",
    )(table, ends, rels, negs, counts)


def far(mask, shard, idx):
    return pl.pallas_call(
        functools.partial(far_kernel, mask),
        out_shape=(shape(shard.shape[0], 4 * LANES), like(shard), like(idx)),
        in_specs=[VMEM] * 2,
        out_specs=(VMEM,) * 3,
        scratch_shapes=[DMA((5,)), DMA((5,)), DMA((1,))],
        compiler_params=params(mask),
        name=f"far_{mask}",
    )(shard, idx)


def near(mask, shard, idx):
    return pl.pallas_call(
        functools.partial(near_kernel, mask),
        out_shape=(shape(shard.shape[0], 4 * LANES), like(idx)),
        in_specs=[VMEM] * 2,
        out_specs=(VMEM,) * 2,
        scratch_shapes=[DMA((9,)), DMA((9,)), DMA((1,))],
        compiler_params=params(16 + mask),
        name=f"near_{mask}",
    )(shard, idx)


def one_round(other, other_idx, own, here_idx, relations, table, state):
    width, rows = own.shape
    low, edges = jnp.bfloat16, 4 * BLOCK
    return pl.pallas_call(
        round_kernel,
        out_shape=(like(table), like(state), like(table, low)),
        in_specs=[VMEM] * 7,
        out_specs=(VMEM,) * 3,
        scratch_shapes=[
            pltpu.VMEM((rows, width), low),
            pltpu.VMEM((rows, width), low),
            pltpu.VMEM((width, edges), low),
            pltpu.VMEM((width, edges), low),
            pltpu.VMEM((width, edges), low),
            pltpu.VMEM((rows, edges), low),
            pltpu.VMEM((rows, edges), low),
            pltpu.VMEM((4, width, LANES), low),
            pltpu.VMEM((3, width, LANES), low),
            DMA((3,)),
            DMA((3,)),
        ],
        compiler_params=params(24),
        name="one_round",
    )(other, other_idx, own, here_idx, relations, table, state)


def on_device(
    embeddings, adagrad_state, relations, endpoints, relation_ids, negatives, edge_counts, plan
):
    table = embeddings.T
    state = adagrad_state[None, :]
    relations = relations.T
    high, low = plan >> LOW_BITS, plan & (2**LOW_BITS - 1)
    shard, *packed = pack(table, endpoints, relation_ids, negatives, edge_counts)
    fars = [functools.partial(far, mask) for mask in range(16)]
    nears = [functools.partial(near, mask) for mask in range(8)]
    for r in range(plan.shape[0]):
        here, away = packed[2 * r : 2 * r + 2]
        own, other, idx = lax.switch(high[r], fars, shard, away)
        other, idx = lax.switch(low[r], nears, other, idx)
        table, state, shard = one_round(other, idx, own, here, relations, table, state)
    return table.T, state[0]


def solution(mesh):
    in_specs = (
        P(("dom", "edge"), None),
        P(("dom", "edge")),
        P(),
        P(None, None, "dom", "edge"),
        P(None, "dom", "edge"),
        P(None, None, "dom", "edge", None),
        P(None, "dom", "edge"),
        P(),
    )
    out_specs = (P(("dom", "edge"), None), P(("dom", "edge")))
    return jax.shard_map(
        on_device, mesh=mesh, in_specs=in_specs, out_specs=out_specs, check_vma=False
    )
```

time: 108 us -> 99.2 us (0.919)
  Pallas kernels: 95.9 us -> 90.2 us
  other arithmetic: 1.5 us -> 0.01 us
  between operations: 4.71 us -> 3.48 us
    pallas_call x6 -> x7, Pallas kernels: 95.9 us -> 90.2 us  [the longest x2 40.2 us: far(): pl.pallas_call(functools.partial(far_kernel, mask), out_shape=(shape(shar...]
    slice x2 -> x1, local copies, waits for them, and re-layouts: 2.63 us -> 0.67 us  [on_device(): own, other, idx = lax.switch(high[r], fars, shard, away)]
    unnamed x13 -> x21, local copies, waits for them, and re-layouts: 2.6 us -> 4.08 us
    add x4 -> x0, other arithmetic: 1.46 us -> none  [the longest x1 0.74 us: packed_edges(): own_ids + other_ids * 65536]
where the time goes in v1:
time: 99.2 us; the launch traced here: 98.8 us
  Pallas kernels  90.2 us (91%)
  local copies, waits for them, and re-layouts  4.75 us (5%)
  between operations  3.48 us (4%)
    pallas_call x2, Pallas kernels, far(): pl.pallas_call(functools.partial(far_kernel, mask), out_shape=(shape(shar...  40.2 us
    pallas_call x2, Pallas kernels, one_round(): pl.pallas_call(round_kernel, out_shape=(like(table), like(state), like(ta...  26.4 us
    pallas_call x2, Pallas kernels, near(): pl.pallas_call(functools.partial(near_kernel, mask), out_shape=(shape(sha...  23.4 us
    unnamed x21, local copies, waits for them, and re-layouts  4.08 us

profile of v1, /device:TPU:1, one launch (start us, length us, event | category | flops | bytes accessed | tf_op | source)
XLA Modules:
  0.0 98.8 jit_solution(7590936714691554868)
XLA Ops:
  0.6 0.0 copy-start.7
  0.6 0.6 copy-done.7
  1.3 0.0 copy-start.8
  1.3 0.1 copy.10.counts
  1.4 0.6 copy-done.8
  1.9 0.7 fusion
  2.6 0.0 copy-start.5
  3.3 0.0 copy-start.4
  3.3 0.0 copy-start.3
  5.3 0.0 copy-done.5
  5.4 0.0 copy-done.4
  5.4 0.0 copy-done.3
  5.4 0.0 copy-start.1
  5.4 0.9 copy-done.1
  6.3 0.1 pack.1
  6.4 24.5 %conditional.4 = ((bf16[400,512]{1,0:T(8,128)(2,1)S(1)}, bf16[400,128]{1,0:T(8,128)(2,1)S(1)}, s32[8,256]{1,0:T(8,128)S(1)})) conditional(s32[]{:T(128)} %bitcast.3, (bf16[400,128]{1,0:T(8,128)(2,1)S(1)}, s32[8,256]{1,0:T(8,128)S(1)}) %tuple.152, (bf16[400,128]{1,0:T(8,128)(2,1)S(1)}, ...), branch_computations={%region_0.0_spmd, %region_1.0_spmd, %region_2.0_spmd, %region_3.0_... | conditional | bytes 8 | solution.py:375
  6.4 24.5 %far_15.2 = (bf16[400,512]{1,0:T(8,128)(2,1)S(1)}, bf16[400,128]{1,0:T(8,128)(2,1)S(1)}, s32[8,256]{1,0:T(8,128)S(1)}) custom-call(bf16[400,128]{1,0:T(8,128)(2,1)S(1)} %get-tuple-element.222.mine, s32[8,256]{1,0:T(8,128)S(1)} %get-tuple-element.223.idx), custom_call_target="tpu_custom_call" | custom-call | tf_op jit(solution)/shard_map/cond/branch_15_fun/far_15/pallas_call | solution.py:314
  30.9 0.0 copy-start
  30.9 0.0 copy-start.2
  30.9 11.7 %conditional.5 = ((bf16[400,512]{1,0:T(8,128)(2,1)S(1)}, s32[8,256]{1,0:T(8,128)S(1)})) conditional(s32[]{:T(128)} %bitcast.2, (bf16[400,128]{1,0:T(8,128)(2,1)S(1)}, s32[8,256]{1,0:T(8,128)S(1)}) %tuple.153, (bf16[400,128]{1,0:T(8,128)(2,1)S(1)}, s32[8,256]{1,0:T(8,128)S(1)}) %tuple.153, ...), branch_computations={%region_16.0_spmd, %region_17.0_spmd, %region_18.0_spmd, %region_1... | conditional | bytes 8 | solution.py:376
  31.0 11.7 %near_7.2 = (bf16[400,512]{1,0:T(8,128)(2,1)S(1)}, s32[8,256]{1,0:T(8,128)S(1)}) custom-call(bf16[400,128]{1,0:T(8,128)(2,1)S(1)} %get-tuple-element.238.shard, s32[8,256]{1,0:T(8,128)S(1)} %get-tuple-element.239.idx), custom_call_target="tpu_custom_call" | custom-call | tf_op jit(solution)/shard_map/cond/branch_7_fun/near_7/pallas_call | solution.py:326
  42.6 0.0 copy-start.6
  42.6 0.0 copy-done
  42.7 0.0 copy-done.2
  42.7 0.6 copy-done.6
  43.3 12.9 %one_round.2 = (f32[400,128]{1,0:T(8,128)S(1)}, f32[1,128]{1,0:T(1,128)S(1)}, bf16[400,128]{1,0:T(8,128)(2,1)S(1)}) custom-call(bf16[400,512]{1,0:T(8,128)(2,1)S(1)} %get-tuple-element.314.other, s32[8,256]{1,0:T(8,128)S(1)} %get-tuple-element.315.other_idx, bf16[400,512]{1,0:T(8,128)(2,1)S(1)} %get-tuple-element.316.own, ...), custom_call_target="tpu_custom_call" | custom-call | tf_op jit(solution)/shard_map/one_round/pallas_call | solution.py:340
  56.2 15.8 %conditional.6 = ((bf16[400,512]{1,0:T(8,128)(2,1)S(1)}, bf16[400,128]{1,0:T(8,128)(2,1)S(1)}, s32[8,256]{1,0:T(8,128)S(1)})) conditional(s32[]{:T(128)} %bitcast.1, (bf16[400,128]{1,0:T(8,128)(2,1)S(1)}, s32[8,256]{1,0:T(8,128)S(1)}) %tuple.154, (bf16[400,128]{1,0:T(8,128)(2,1)S(1)}, ...), branch_computations={%region_24.0_spmd, %region_25.0_spmd, %region_26.0_spmd, %region_2... | conditional | bytes 8 | solution.py:375
  56.2 15.8 %far_4.3 = (bf16[400,512]{1,0:T(8,128)(2,1)S(1)}, bf16[400,128]{1,0:T(8,128)(2,1)S(1)}, s32[8,256]{1,0:T(8,128)S(1)}) custom-call(bf16[400,128]{1,0:T(8,128)(2,1)S(1)} %get-tuple-element.248.mine, s32[8,256]{1,0:T(8,128)S(1)} %get-tuple-element.249.idx), custom_call_target="tpu_custom_call" | custom-call | tf_op jit(solution)/shard_map/cond/branch_4_fun/far_4/pallas_call | solution.py:314
  72.0 12.0 %conditional.7 = ((bf16[400,512]{1,0:T(8,128)(2,1)S(1)}, s32[8,256]{1,0:T(8,128)S(1)})) conditional(s32[]{:T(128)} %bitcast, (bf16[400,128]{1,0:T(8,128)(2,1)S(1)}, s32[8,256]{1,0:T(8,128)S(1)}) %tuple.155, (bf16[400,128]{1,0:T(8,128)(2,1)S(1)}, s32[8,256]{1,0:T(8,128)S(1)}) %tuple.155, ...), branch_computations={%region_40.0_spmd, %region_41.0_spmd, %region_42.0_spmd, %region_4... | conditional | bytes 8 | solution.py:376
  72.1 11.8 %near_5.3 = (bf16[400,512]{1,0:T(8,128)(2,1)S(1)}, s32[8,256]{1,0:T(8,128)S(1)}) custom-call(bf16[400,128]{1,0:T(8,128)(2,1)S(1)} %get-tuple-element.282.shard, s32[8,256]{1,0:T(8,128)S(1)} %get-tuple-element.283.idx), custom_call_target="tpu_custom_call" | custom-call | tf_op jit(solution)/shard_map/cond/branch_5_fun/near_5/pallas_call | solution.py:326
  84.0 13.5 %one_round.3 = (f32[400,128]{1,0:T(8,128)S(1)}, f32[1,128]{1,0:T(1,128)S(1)}, bf16[400,128]{1,0:T(8,128)(2,1)}) custom-call(bf16[400,512]{1,0:T(8,128)(2,1)S(1)} %get-tuple-element.322.other, s32[8,256]{1,0:T(8,128)S(1)} %get-tuple-element.323.other_idx, bf16[400,512]{1,0:T(8,128)(2,1)S(1)} %get-tuple-element.324.own, ...), custom_call_target="tpu_custom_call" | custom-call | tf_op jit(solution)/shard_map/one_round/pallas_call | solution.py:340
  97.6 0.7 copy.141
  98.3 0.5 copy.142
  (1 shorter events, 0.0 us)
Async XLA Ops:
  0.6 0.7 copy-start.7
  1.3 0.7 copy-start.8
  2.6 2.7 %copy-start.5 = (s32[2,1,512]{2,1,0:T(1,128)S(1)}, s32[2,1,512]{2,1,0:T(1,128)}, u32[]{:S(2)}) copy-start(s32[2,1,512]{2,1,0:T(1,128)} %rels.1) | copy-start | bytes 12292
  3.3 2.0 %copy-start.4 = (s32[2,2,1,2,256]{4,3,2,1,0:T(2,128)S(1)}, s32[2,2,1,2,256]{4,3,2,1,0:T(2,128)}, u32[]{:S(2)}) copy-start(s32[2,2,1,2,256]{4,3,2,1,0:T(2,128)} %negs.1) | copy-start | bytes 24580
  3.3 2.0 %copy-start.3 = (s32[2,2,1,512]{3,2,1,0:T(1,128)S(1)}, s32[2,2,1,512]{3,2,1,0:T(1,128)}, u32[]{:S(2)}) copy-start(s32[2,2,1,512]{3,2,1,0:T(1,128)} %ends.1) | copy-start | bytes 24580
  5.4 0.9 copy-start.1
  30.9 11.7 %copy-start = (bf16[256,400]{0,1:T(8,128)(2,1)S(1)}, bf16[256,400]{0,1:T(8,128)(2,1)}, u32[]{:S(2)}) copy-start(bf16[256,400]{0,1:T(8,128)(2,1)} %param.58) | copy-start | bytes 614404
  30.9 11.7 %copy-start.2 = (f32[128,400]{0,1:T(8,128)S(1)}, f32[128,400]{0,1:T(8,128)}, u32[]{:S(2)}) copy-start(f32[128,400]{0,1:T(8,128)} %param.56) | copy-start | bytes 614404
  42.6 0.7 copy-start.6

commit v2 on v1

--- a/solution.py
+++ b/solution.py
@@ -73,12 +73,24 @@
         copy.wait()
 
 
-def pack_kernel(table, ends, rels, negs, counts, shard, *packed):
-    shard[...] = table[...].astype(jnp.bfloat16)
+def pack_kernel(*refs):
+    given, (table_out, state_out, shard), packed = refs[:6], refs[6:9], refs[9:13]
+    fetched, done = refs[13:17], refs[17]
+    places = (table_out, state_out) + fetched
+    copies = [
+        pltpu.make_async_copy(src, dst, done.at[k])
+        for k, (src, dst) in enumerate(zip(given, places))
+    ]
+    for copy in copies:
+        copy.start()
+    for copy in copies:
+        copy.wait()
+    ends, rels, negs, counts = fetched
+    shard[...] = table_out[...].astype(jnp.bfloat16)
     for r in range(2):
         here, away = packed[2 * r : 2 * r + 2]
         left, right = ends[r, 0], ends[r, 1]
-        rel = rels[r] + counts[r] * 65536
+        rel = rels[r] + counts[:, r : r + 1] * 65536
         there, back = left + right * 65536, right + left * 65536
         for half in range(2):
             at = slice(half * BLOCK, (half + 1) * BLOCK)
@@ -168,18 +180,14 @@
 def round_kernel(
     other, other_idx, own, here_idx, relations, table, state,
     table_out, state_out, shard_out,
-    own_rows, other_rows, rel_kept, factors, grads, pick_own, weights_own, parts, arrived,
+    own_rows, other_rows, rel_kept, factors, grads, pick_own, weights_own, totals, parts, chip_sum, arrived,
     send, recv,
 ):
     dom, edge = lax.axis_index("dom"), lax.axis_index("edge")
     chip, core = edge // 2, edge % 2
     sibling = (dom, chip * 2 + (1 - core))
-    mates = [
-        (dom, (1 - chip) * 2 + core),
-        (dom, (1 - chip) * 2 + (1 - core)),
-        sibling,
-    ]
-    greet(mates)
+    across = (dom, (1 - chip) * 2 + core)
+    greet([across, sibling])
     width, rows = own.shape
 
     def ids_of(b, kind):
@@ -240,36 +248,38 @@
         own_side(b)
         both_sides(b)
 
-    def partial(which):
+    def partial(which, kept):
         at = pl.ds(pl.multiple_of(which * BLOCK, BLOCK), BLOCK)
         total = across_rows(grads[...], pick_own[at, :]) + across_rows(
             factors[...], weights_own[at, :]
         )
-        total = total.astype(jnp.bfloat16)
-        parts[2 * which] = total[:, :LANES]
-        parts[2 * which + 1] = total[:, LANES:]
+        for c in range(2):
+            half = total[:, c * LANES : (c + 1) * LANES]
+            totals[kept, c] = half
+            parts[kept, c] = half.astype(jnp.bfloat16)
+
+    def given(src, at, device):
+        return pltpu.make_async_remote_copy(
+            src, arrived.at[at], send.at[at], recv.at[at], device_id=device, device_id_type=MESH
+        )
 
     gifts = [
-        pltpu.make_async_remote_copy(
-            parts.at[mate[1]],
-            arrived.at[k],
-            send.at[k],
-            recv.at[k],
-            device_id=mate,
-            device_id_type=MESH,
-        )
-        for k, mate in enumerate(mates)
+        given(parts.at[0, 1 - core], 0, sibling),
+        given(parts.at[1, 1 - core], 1, sibling),
+        given(chip_sum, 2, across),
     ]
-    partial(1 - chip)
-    greeted(3)
+    partial(1 - chip, 0)
+    greeted(2)
     gifts[0].start()
+    partial(chip, 1)
     gifts[1].start()
-    partial(chip)
+    gifts[0].wait_recv()
+    chip_sum[...] = (totals[0, core] + arrived[0].astype(jnp.float32)).astype(jnp.bfloat16)
     gifts[2].start()
-    grad = parts[edge].astype(jnp.float32)
-    for k in (2, 0, 1):
-        gifts[k].wait_recv()
-        grad = grad + arrived[k].astype(jnp.float32)
+    gifts[1].wait_recv()
+    grad = totals[1, core] + arrived[1].astype(jnp.float32)
+    gifts[2].wait_recv()
+    grad = grad + arrived[2].astype(jnp.float32)
     new_state = state[...] + jnp.sum(grad * grad, axis=0, keepdims=True) * (1.0 / width)
     new_table = table[...] - learning_rate * grad / jnp.sqrt(new_state)
     shard_out[...] = new_table.astype(jnp.bfloat16)
@@ -298,16 +308,34 @@
     )
 
 
-def pack(table, ends, rels, negs, counts):
+def pack(table, state, ends, rels, negs, counts):
     idx = shape(8, BLOCK, dtype=jnp.int32)
+    rest = (ends, rels, negs, counts)
     return pl.pallas_call(
         pack_kernel,
-        out_shape=(like(table, jnp.bfloat16),) + (idx,) * 4,
-        in_specs=[VMEM] * 5,
-        out_specs=(VMEM,) * 5,
+        out_shape=(like(table), like(state), like(table, jnp.bfloat16)) + (idx,) * 4,
+        in_specs=[pl.BlockSpec(memory_space=pl.ANY)] * 6,
+        out_specs=(VMEM,) * 7,
+        scratch_shapes=[pltpu.VMEM(a.shape, a.dtype) for a in rest] + [DMA((6,))],
         compiler_params=pltpu.CompilerParams(vmem_limit_bytes=LIMIT),
         name="pack",
-    )(table, ends, rels, negs, counts)
+    )(table, state, *rest)
+
+
+def hand_over_kernel(table, state, table_out, state_out):
+    table_out[...] = table[...]
+    state_out[...] = state[...]
+
+
+def hand_over(table, state):
+    return pl.pallas_call(
+        hand_over_kernel,
+        out_shape=(like(table), like(state)),
+        in_specs=[VMEM] * 2,
+        out_specs=(VMEM,) * 2,
+        compiler_params=pltpu.CompilerParams(vmem_limit_bytes=LIMIT),
+        name="hand_over",
+    )(table, state)
 
 
 def far(mask, shard, idx):
@@ -350,7 +378,9 @@
             pltpu.VMEM((width, edges), low),
             pltpu.VMEM((rows, edges), low),
             pltpu.VMEM((rows, edges), low),
-            pltpu.VMEM((4, width, LANES), low),
+            pltpu.VMEM((2, 2, width, LANES), jnp.float32),
+            pltpu.VMEM((2, 2, width, LANES), low),
+            pltpu.VMEM((width, LANES), low),
             pltpu.VMEM((3, width, LANES), low),
             DMA((3,)),
             DMA((3,)),
@@ -367,7 +397,9 @@
     state = adagrad_state[None, :]
     relations = relations.T
     high, low = plan >> LOW_BITS, plan & (2**LOW_BITS - 1)
-    shard, *packed = pack(table, endpoints, relation_ids, negatives, edge_counts)
+    table, state, shard, *packed = pack(
+        table, state, endpoints, relation_ids, negatives, edge_counts.reshape(1, -1)
+    )
     fars = [functools.partial(far, mask) for mask in range(16)]
     nears = [functools.partial(near, mask) for mask in range(8)]
     for r in range(plan.shape[0]):
@@ -375,6 +407,7 @@
         own, other, idx = lax.switch(high[r], fars, shard, away)
         other, idx = lax.switch(low[r], nears, other, idx)
         table, state, shard = one_round(other, idx, own, here, relations, table, state)
+    table, state = hand_over(table, state)
     return table.T, state[0]
 
 

time: 99.2 us -> 85.2 us (0.86)
  Pallas kernels: 90.2 us -> 78.1 us
  local copies, waits for them, and re-layouts: 4.75 us -> 2.9 us
    pallas_call x2, Pallas kernels: 40.2 us -> 34.3 us  [far(): pl.pallas_call(functools.partial(far_kernel, mask), out_shape=(shape(shar...]
    pallas_call x2, Pallas kernels: 23.4 us -> 18.8 us  [near(): pl.pallas_call(functools.partial(near_kernel, mask), out_shape=(shape(sha...]
    pallas_call x2, Pallas kernels: 26.4 us -> 23.9 us  [one_round(): pl.pallas_call(round_kernel, out_shape=(like(table), like(state), like(ta...]
    unnamed x21 -> x16, local copies, waits for them, and re-layouts: 4.08 us -> 2.23 us
    pallas_call x1 -> x2, Pallas kernels: 0.08 us -> 1.1 us  [the longest x1 0.7 us: hand_over(): pl.pallas_call(hand_over_kernel, out_shape=(like(table), like(state)), in...]
where the time goes in v2:
time: 85.2 us; the launch traced here: 84.8 us
  Pallas kernels  78.1 us (92%)
  between operations  3.47 us (4%)
  local copies, waits for them, and re-layouts  2.9 us (3%)
    pallas_call x2, Pallas kernels, far(): pl.pallas_call(functools.partial(far_kernel, mask), out_shape=(shape(shar...  34.3 us
    pallas_call x2, Pallas kernels, one_round(): pl.pallas_call(round_kernel, out_shape=(like(table), like(state), like(ta...  23.9 us
    pallas_call x2, Pallas kernels, near(): pl.pallas_call(functools.partial(near_kernel, mask), out_shape=(shape(sha...  18.8 us
    unnamed x16, local copies, waits for them, and re-layouts  2.23 us

profile of v2, /device:TPU:1, one launch (start us, length us, event | category | flops | bytes accessed | tf_op | source)
XLA Modules:
  0.0 84.8 jit_solution(10230626219725679217)
XLA Ops:
  0.6 0.0 copy-start.7
  0.6 0.6 copy-done.7
  1.3 0.7 fusion
  2.0 0.0 copy-start.4
  2.7 0.0 copy-start.3
  2.7 0.0 copy-start.2
  4.7 0.0 copy-start.5
  4.7 0.0 copy-start.6
  4.7 0.0 copy-done.4
  4.7 0.0 copy-done.3
  4.7 0.0 copy-done.2
  4.7 0.6 copy-done.5
  5.3 0.0 copy-done.6
  5.4 0.0 copy-start.1
  5.4 0.9 %copy-done.1 = f32[128,400]{0,1:T(8,128)S(1)} copy-done((f32[128,400]{0,1:T(8,128)S(1)}, f32[128,400]{0,1:T(8,128)}, u32[]{:S(2)}) %copy-start.1) | copy-done | bytes 204824
  6.3 0.4 pack.1
  6.7 24.5 %conditional.4 = ((bf16[400,512]{1,0:T(8,128)(2,1)S(1)}, bf16[400,128]{1,0:T(8,128)(2,1)S(1)}, s32[8,256]{1,0:T(8,128)S(1)})) conditional(s32[]{:T(128)} %bitcast.3, (bf16[400,128]{1,0:T(8,128)(2,1)S(1)}, s32[8,256]{1,0:T(8,128)S(1)}) %tuple.152, (bf16[400,128]{1,0:T(8,128)(2,1)S(1)}, ...), branch_computations={%region_0.0_spmd, %region_1.0_spmd, %region_2.0_spmd, %region_3.0_... | conditional | bytes 8 | solution.py:407
  6.8 24.5 %far_15.2 = (bf16[400,512]{1,0:T(8,128)(2,1)S(1)}, bf16[400,128]{1,0:T(8,128)(2,1)S(1)}, s32[8,256]{1,0:T(8,128)S(1)}) custom-call(bf16[400,128]{1,0:T(8,128)(2,1)S(1)} %get-tuple-element.222.mine, s32[8,256]{1,0:T(8,128)S(1)} %get-tuple-element.223.idx), custom_call_target="tpu_custom_call" | custom-call | tf_op jit(solution)/shard_map/cond/branch_15_fun/far_15/pallas_call | solution.py:342
  31.3 0.0 copy-start
  31.3 11.7 %conditional.5 = ((bf16[400,512]{1,0:T(8,128)(2,1)S(1)}, s32[8,256]{1,0:T(8,128)S(1)})) conditional(s32[]{:T(128)} %bitcast.2, (bf16[400,128]{1,0:T(8,128)(2,1)S(1)}, s32[8,256]{1,0:T(8,128)S(1)}) %tuple.153, (bf16[400,128]{1,0:T(8,128)(2,1)S(1)}, s32[8,256]{1,0:T(8,128)S(1)}) %tuple.153, ...), branch_computations={%region_16.0_spmd, %region_17.0_spmd, %region_18.0_spmd, %region_1... | conditional | bytes 8 | solution.py:408
  31.3 11.7 %near_7.2 = (bf16[400,512]{1,0:T(8,128)(2,1)S(1)}, s32[8,256]{1,0:T(8,128)S(1)}) custom-call(bf16[400,128]{1,0:T(8,128)(2,1)S(1)} %get-tuple-element.238.shard, s32[8,256]{1,0:T(8,128)S(1)} %get-tuple-element.239.idx), custom_call_target="tpu_custom_call" | custom-call | tf_op jit(solution)/shard_map/cond/branch_7_fun/near_7/pallas_call | solution.py:354
  43.0 0.0 copy-done
  43.0 11.8 %one_round.2 = (f32[400,128]{1,0:T(8,128)S(1)}, f32[1,128]{1,0:T(1,128)S(1)}, bf16[400,128]{1,0:T(8,128)(2,1)S(1)}) custom-call(bf16[400,512]{1,0:T(8,128)(2,1)S(1)} %get-tuple-element.318.other, s32[8,256]{1,0:T(8,128)S(1)} %get-tuple-element.319.other_idx, bf16[400,512]{1,0:T(8,128)(2,1)S(1)} %get-tuple-element.320.own, ...), custom_call_target="tpu_custom_call" | custom-call | tf_op jit(solution)/shard_map/one_round/pallas_call | solution.py:368
  54.8 9.9 %conditional.6 = ((bf16[400,512]{1,0:T(8,128)(2,1)S(1)}, bf16[400,128]{1,0:T(8,128)(2,1)S(1)}, s32[8,256]{1,0:T(8,128)S(1)})) conditional(s32[]{:T(128)} %bitcast.1, (bf16[400,128]{1,0:T(8,128)(2,1)S(1)}, s32[8,256]{1,0:T(8,128)S(1)}) %tuple.154, (bf16[400,128]{1,0:T(8,128)(2,1)S(1)}, ...), branch_computations={%region_24.0_spmd, %region_25.0_spmd, %region_26.0_spmd, %region_2... | conditional | bytes 8 | solution.py:407
  54.8 9.8 %far_2.3 = (bf16[400,512]{1,0:T(8,128)(2,1)S(1)}, bf16[400,128]{1,0:T(8,128)(2,1)S(1)}, s32[8,256]{1,0:T(8,128)S(1)}) custom-call(bf16[400,128]{1,0:T(8,128)(2,1)S(1)} %get-tuple-element.244.mine, s32[8,256]{1,0:T(8,128)S(1)} %get-tuple-element.245.idx), custom_call_target="tpu_custom_call" | custom-call | tf_op jit(solution)/shard_map/cond/branch_2_fun/far_2/pallas_call | solution.py:342
  64.7 7.3 %conditional.7 = ((bf16[400,512]{1,0:T(8,128)(2,1)S(1)}, s32[8,256]{1,0:T(8,128)S(1)})) conditional(s32[]{:T(128)} %bitcast, (bf16[400,128]{1,0:T(8,128)(2,1)S(1)}, s32[8,256]{1,0:T(8,128)S(1)}) %tuple.155, (bf16[400,128]{1,0:T(8,128)(2,1)S(1)}, s32[8,256]{1,0:T(8,128)S(1)}) %tuple.155, ...), branch_computations={%region_40.0_spmd, %region_41.0_spmd, %region_42.0_spmd, %region_4... | conditional | bytes 8 | solution.py:408
  64.7 7.1 %near_1.3 = (bf16[400,512]{1,0:T(8,128)(2,1)S(1)}, s32[8,256]{1,0:T(8,128)S(1)}) custom-call(bf16[400,128]{1,0:T(8,128)(2,1)S(1)} %get-tuple-element.274.shard, s32[8,256]{1,0:T(8,128)S(1)} %get-tuple-element.275.idx), custom_call_target="tpu_custom_call" | custom-call | tf_op jit(solution)/shard_map/cond/branch_1_fun/near_1/pallas_call | solution.py:354
  72.0 12.1 %one_round.3 = (f32[400,128]{1,0:T(8,128)S(1)}, f32[1,128]{1,0:T(1,128)S(1)}, bf16[400,128]{1,0:T(8,128)(2,1)}) custom-call(bf16[400,512]{1,0:T(8,128)(2,1)S(1)} %get-tuple-element.328.other, s32[8,256]{1,0:T(8,128)S(1)} %get-tuple-element.329.other_idx, bf16[400,512]{1,0:T(8,128)(2,1)S(1)} %get-tuple-element.330.own, ...), custom_call_target="tpu_custom_call" | custom-call | tf_op jit(solution)/shard_map/one_round/pallas_call | solution.py:368
  84.1 0.7 hand_over.1
  (1 shorter events, 0.0 us)
Async XLA Ops:
  0.6 0.7 copy-start.7
  2.0 2.8 %copy-start.4 = (s32[2,1,512]{2,1,0:T(1,128)S(1)}, s32[2,1,512]{2,1,0:T(1,128)}, u32[]{:S(2)}) copy-start(s32[2,1,512]{2,1,0:T(1,128)} %refs_3_.1) | copy-start | bytes 12292
  2.7 2.1 %copy-start.3 = (s32[2,2,1,2,256]{4,3,2,1,0:T(2,128)S(1)}, s32[2,2,1,2,256]{4,3,2,1,0:T(2,128)}, u32[]{:S(2)}) copy-start(s32[2,2,1,2,256]{4,3,2,1,0:T(2,128)} %refs_4_.1) | copy-start | bytes 24580
  2.7 2.1 %copy-start.2 = (s32[2,2,1,512]{3,2,1,0:T(1,128)S(1)}, s32[2,2,1,512]{3,2,1,0:T(1,128)}, u32[]{:S(2)}) copy-start(s32[2,2,1,512]{3,2,1,0:T(1,128)} %refs_2_.1) | copy-start | bytes 24580
  4.7 0.7 copy-start.5
  4.7 0.7 copy-start.6
  5.4 0.9 %copy-start.1 = (f32[128,400]{0,1:T(8,128)S(1)}, f32[128,400]{0,1:T(8,128)}, u32[]{:S(2)}) copy-start(f32[128,400]{0,1:T(8,128)} %param.56) | copy-start | bytes 614404
  31.3 11.7 %copy-start = (bf16[256,400]{0,1:T(8,128)(2,1)S(1)}, bf16[256,400]{0,1:T(8,128)(2,1)}, u32[]{:S(2)}) copy-start(bf16[256,400]{0,1:T(8,128)(2,1)} %param.58) | copy-start | bytes 614404

commit v3 on v2

--- a/solution.py
+++ b/solution.py
@@ -14,6 +14,9 @@
 BLOCK = 256
 
 
+CHUNKS = ((0, 208), (208, 192))
+
+
 def xor(value, mask):
     out = value
     for bit in range(mask.bit_length()):
@@ -40,13 +43,14 @@
     dom, edge = lax.axis_index("dom"), lax.axis_index("edge")
     mates = [(dom, (edge + k) % 4) for k in range(1, 4)]
     across = (xor(dom, mask << LOW_BITS), edge)
-    greet(mates + ([across] if mask else []))
+    greet(([across] if mask else []) + mates)
     kept = pltpu.make_async_copy(mine, own_full.at[:, columns(edge)], local.at[0])
     kept.start()
     greeted(4 if mask else 3)
     copies = []
     if mask:
-        for at, (src, dst) in enumerate(((mine, other), (idx, other_idx))):
+        pieces = [(mine.at[pl.ds(*c), :], other.at[pl.ds(*c), :]) for c in CHUNKS]
+        for at, (src, dst) in enumerate(pieces + [(idx, other_idx)]):
             copies.append(
                 pltpu.make_async_remote_copy(
                     src, dst, send.at[at], recv.at[at], device_id=across, device_id_type=MESH
@@ -57,8 +61,8 @@
             pltpu.make_async_remote_copy(
                 mine,
                 own_full.at[:, columns(edge)],
-                send.at[2 + k],
-                recv.at[2 + k],
+                send.at[3 + k],
+                recv.at[3 + k],
                 device_id=mate,
                 device_id_type=MESH,
             )
@@ -124,16 +128,13 @@
     return jnp.where(condition, 1.0, 0.0)
 
 
-CHUNKS = ((0, 208), (208, 192))
-
-
 def near_kernel(mask, shard, idx, full, full_idx, send, recv, local):
     dom, edge = lax.axis_index("dom"), lax.axis_index("edge")
     chip, core = edge // 2, edge % 2
     partner = xor(dom, mask)
     other = (1 - chip) * 2 + core
     straight, crossed, sibling = (partner, edge), (partner, other), (dom, chip * 2 + (1 - core))
-    greet([crossed, sibling] + ([straight] if mask else []))
+    greet(([straight] if mask else []) + [crossed, sibling])
     if not mask:
         kept = pltpu.make_async_copy(shard, full.at[:, columns(edge)], local.at[0])
         kept.start()
@@ -344,7 +345,7 @@
         out_shape=(shape(shard.shape[0], 4 * LANES), like(shard), like(idx)),
         in_specs=[VMEM] * 2,
         out_specs=(VMEM,) * 3,
-        scratch_shapes=[DMA((5,)), DMA((5,)), DMA((1,))],
+        scratch_shapes=[DMA((6,)), DMA((6,)), DMA((1,))],
         compiler_params=params(mask),
         name=f"far_{mask}",
     )(shard, idx)

time: 85.2 us -> 96.6 us (1.13)
  Pallas kernels: 78.1 us -> 89.4 us
    pallas_call x2, Pallas kernels: 18.8 us -> 30.7 us  [near(): pl.pallas_call(functools.partial(near_kernel, mask), out_shape=(shape(sha...]
where the time goes in v3:
time: 96.6 us; the launch traced here: 96.2 us
  Pallas kernels  89.4 us (93%)
  between operations  3.47 us (4%)
  local copies, waits for them, and re-layouts  2.9 us (3%)
    pallas_call x2, Pallas kernels, far(): pl.pallas_call(functools.partial(far_kernel, mask), out_shape=(shape(shar...  33.4 us
    pallas_call x2, Pallas kernels, near(): pl.pallas_call(functools.partial(near_kernel, mask), out_shape=(shape(sha...  30.7 us
    pallas_call x2, Pallas kernels, one_round(): pl.pallas_call(round_kernel, out_shape=(like(table), like(state), like(ta...  24.2 us
    unnamed x16, local copies, waits for them, and re-layouts  2.23 us

profile of v3, /device:TPU:1, one launch (start us, length us, event | category | flops | bytes accessed | tf_op | source)
XLA Modules:
  0.0 96.2 jit_solution(608323069245623811)
XLA Ops:
  0.6 0.0 copy-start.7
  0.6 0.6 copy-done.7
  1.3 0.7 fusion
  2.0 0.0 copy-start.4
  2.7 0.0 copy-start.3
  2.7 0.0 copy-start.2
  4.7 0.0 copy-start.5
  4.7 0.0 copy-start.6
  4.7 0.0 copy-done.4
  4.7 0.0 copy-done.3
  4.7 0.0 copy-done.2
  4.7 0.6 copy-done.5
  5.3 0.0 copy-done.6
  5.4 0.0 copy-start.1
  5.4 0.9 copy-done.1
  6.3 0.4 pack.1
  6.7 23.2 %conditional.4 = ((bf16[400,512]{1,0:T(8,128)(2,1)S(1)}, bf16[400,128]{1,0:T(8,128)(2,1)S(1)}, s32[8,256]{1,0:T(8,128)S(1)})) conditional(s32[]{:T(128)} %bitcast.3, (bf16[400,128]{1,0:T(8,128)(2,1)S(1)}, s32[8,256]{1,0:T(8,128)S(1)}) %tuple.152, (bf16[400,128]{1,0:T(8,128)(2,1)S(1)}, ...), branch_computations={%region_0.0_spmd, %region_1.0_spmd, %region_2.0_spmd, %region_3.0_... | conditional | bytes 8 | solution.py:408
  6.8 23.1 %far_9.2 = (bf16[400,512]{1,0:T(8,128)(2,1)S(1)}, bf16[400,128]{1,0:T(8,128)(2,1)S(1)}, s32[8,256]{1,0:T(8,128)S(1)}) custom-call(bf16[400,128]{1,0:T(8,128)(2,1)S(1)} %get-tuple-element.210.mine, s32[8,256]{1,0:T(8,128)S(1)} %get-tuple-element.211.idx), custom_call_target="tpu_custom_call" | custom-call | tf_op jit(solution)/shard_map/cond/branch_9_fun/far_9/pallas_call | solution.py:343
  29.9 0.0 copy-start
  29.9 13.0 %conditional.5 = ((bf16[400,512]{1,0:T(8,128)(2,1)S(1)}, s32[8,256]{1,0:T(8,128)S(1)})) conditional(s32[]{:T(128)} %bitcast.2, (bf16[400,128]{1,0:T(8,128)(2,1)S(1)}, s32[8,256]{1,0:T(8,128)S(1)}) %tuple.153, (bf16[400,128]{1,0:T(8,128)(2,1)S(1)}, s32[8,256]{1,0:T(8,128)S(1)}) %tuple.153, ...), branch_computations={%region_16.0_spmd, %region_17.0_spmd, %region_18.0_spmd, %region_1... | conditional | bytes 8 | solution.py:409
  30.0 13.0 %near_3.2 = (bf16[400,512]{1,0:T(8,128)(2,1)S(1)}, s32[8,256]{1,0:T(8,128)S(1)}) custom-call(bf16[400,128]{1,0:T(8,128)(2,1)S(1)} %get-tuple-element.230.shard, s32[8,256]{1,0:T(8,128)S(1)} %get-tuple-element.231.idx), custom_call_target="tpu_custom_call" | custom-call | tf_op jit(solution)/shard_map/cond/branch_3_fun/near_3/pallas_call | solution.py:355
  42.9 0.0 copy-done
  43.0 11.7 %one_round.2 = (f32[400,128]{1,0:T(8,128)S(1)}, f32[1,128]{1,0:T(1,128)S(1)}, bf16[400,128]{1,0:T(8,128)(2,1)S(1)}) custom-call(bf16[400,512]{1,0:T(8,128)(2,1)S(1)} %get-tuple-element.318.other, s32[8,256]{1,0:T(8,128)S(1)} %get-tuple-element.319.other_idx, bf16[400,512]{1,0:T(8,128)(2,1)S(1)} %get-tuple-element.320.own, ...), custom_call_target="tpu_custom_call" | custom-call | tf_op jit(solution)/shard_map/one_round/pallas_call | solution.py:369
  54.7 10.4 %conditional.6 = ((bf16[400,512]{1,0:T(8,128)(2,1)S(1)}, bf16[400,128]{1,0:T(8,128)(2,1)S(1)}, s32[8,256]{1,0:T(8,128)S(1)})) conditional(s32[]{:T(128)} %bitcast.1, (bf16[400,128]{1,0:T(8,128)(2,1)S(1)}, s32[8,256]{1,0:T(8,128)S(1)}) %tuple.154, (bf16[400,128]{1,0:T(8,128)(2,1)S(1)}, ...), branch_computations={%region_24.0_spmd, %region_25.0_spmd, %region_26.0_spmd, %region_2... | conditional | bytes 8 | solution.py:408
  54.8 10.3 %far_15.3 = (bf16[400,512]{1,0:T(8,128)(2,1)S(1)}, bf16[400,128]{1,0:T(8,128)(2,1)S(1)}, s32[8,256]{1,0:T(8,128)S(1)}) custom-call(bf16[400,128]{1,0:T(8,128)(2,1)S(1)} %get-tuple-element.270.mine, s32[8,256]{1,0:T(8,128)S(1)} %get-tuple-element.271.idx), custom_call_target="tpu_custom_call" | custom-call | tf_op jit(solution)/shard_map/cond/branch_15_fun/far_15/pallas_call | solution.py:343
  65.1 17.9 %conditional.7 = ((bf16[400,512]{1,0:T(8,128)(2,1)S(1)}, s32[8,256]{1,0:T(8,128)S(1)})) conditional(s32[]{:T(128)} %bitcast, (bf16[400,128]{1,0:T(8,128)(2,1)S(1)}, s32[8,256]{1,0:T(8,128)S(1)}) %tuple.155, (bf16[400,128]{1,0:T(8,128)(2,1)S(1)}, s32[8,256]{1,0:T(8,128)S(1)}) %tuple.155, ...), branch_computations={%region_40.0_spmd, %region_41.0_spmd, %region_42.0_spmd, %region_4... | conditional | bytes 8 | solution.py:409
  65.3 17.7 %near_7.3 = (bf16[400,512]{1,0:T(8,128)(2,1)S(1)}, s32[8,256]{1,0:T(8,128)S(1)}) custom-call(bf16[400,128]{1,0:T(8,128)(2,1)S(1)} %get-tuple-element.286.shard, s32[8,256]{1,0:T(8,128)S(1)} %get-tuple-element.287.idx), custom_call_target="tpu_custom_call" | custom-call | tf_op jit(solution)/shard_map/cond/branch_7_fun/near_7/pallas_call | solution.py:355
  83.0 12.5 %one_round.3 = (f32[400,128]{1,0:T(8,128)S(1)}, f32[1,128]{1,0:T(1,128)S(1)}, bf16[400,128]{1,0:T(8,128)(2,1)}) custom-call(bf16[400,512]{1,0:T(8,128)(2,1)S(1)} %get-tuple-element.328.other, s32[8,256]{1,0:T(8,128)S(1)} %get-tuple-element.329.other_idx, bf16[400,512]{1,0:T(8,128)(2,1)S(1)} %get-tuple-element.330.own, ...), custom_call_target="tpu_custom_call" | custom-call | tf_op jit(solution)/shard_map/one_round/pallas_call | solution.py:369
  95.5 0.7 hand_over.1
  (1 shorter events, 0.0 us)
Async XLA Ops:
  0.6 0.7 copy-start.7
  2.0 2.8 %copy-start.4 = (s32[2,1,512]{2,1,0:T(1,128)S(1)}, s32[2,1,512]{2,1,0:T(1,128)}, u32[]{:S(2)}) copy-start(s32[2,1,512]{2,1,0:T(1,128)} %refs_3_.1) | copy-start | bytes 12292
  2.7 2.1 %copy-start.3 = (s32[2,2,1,2,256]{4,3,2,1,0:T(2,128)S(1)}, s32[2,2,1,2,256]{4,3,2,1,0:T(2,128)}, u32[]{:S(2)}) copy-start(s32[2,2,1,2,256]{4,3,2,1,0:T(2,128)} %refs_4_.1) | copy-start | bytes 24580
  2.7 2.1 %copy-start.2 = (s32[2,2,1,512]{3,2,1,0:T(1,128)S(1)}, s32[2,2,1,512]{3,2,1,0:T(1,128)}, u32[]{:S(2)}) copy-start(s32[2,2,1,512]{3,2,1,0:T(1,128)} %refs_2_.1) | copy-start | bytes 24580
  4.7 0.7 copy-start.5
  4.7 0.7 copy-start.6
  5.4 0.9 copy-start.1
  29.9 13.0 %copy-start = (bf16[256,400]{0,1:T(8,128)(2,1)S(1)}, bf16[256,400]{0,1:T(8,128)(2,1)}, u32[]{:S(2)}) copy-start(bf16[256,400]{0,1:T(8,128)(2,1)} %param.58) | copy-start | bytes 614404

commit v4 on v3

--- a/solution.py
+++ b/solution.py
@@ -152,7 +152,7 @@
     away = [
         [
             moved(shard.at[pl.ds(*CHUNKS[piece]), :], chunk(full, piece, edge), 2 * piece + k, device)
-            for k, device in enumerate((crossed, straight) if mask else (crossed,))
+            for k, device in enumerate((straight, crossed) if mask else (crossed,))
         ]
         for piece in range(2)
     ]
@@ -165,7 +165,7 @@
     for piece in range(2):
         for k, copy in enumerate(away[piece]):
             copy.wait_recv()
-            here = chunk(full, piece, edge if k else other)
+            here = chunk(full, piece, edge if mask and k == 0 else other)
             forwards.append(moved(here, here, 4 + 2 * piece + k, sibling))
             forwards[-1].start()
         if not mask:

time: 96.6 us -> 93.3 us (0.966)
  Pallas kernels: 89.4 us -> 86.2 us
    pallas_call x2, Pallas kernels: 30.7 us -> 23.7 us  [near(): pl.pallas_call(functools.partial(near_kernel, mask), out_shape=(shape(sha...]
    pallas_call x2, Pallas kernels: 33.4 us -> 37.7 us  [far(): pl.pallas_call(functools.partial(far_kernel, mask), out_shape=(shape(shar...]
where the time goes in v4:
time: 93.3 us; the launch traced here: 93 us
  Pallas kernels  86.2 us (92%)
  between operations  3.47 us (4%)
  local copies, waits for them, and re-layouts  2.9 us (3%)
    pallas_call x2, Pallas kernels, far(): pl.pallas_call(functools.partial(far_kernel, mask), out_shape=(shape(shar...  37.7 us
    pallas_call x2, Pallas kernels, near(): pl.pallas_call(functools.partial(near_kernel, mask), out_shape=(shape(sha...  23.7 us
    pallas_call x2, Pallas kernels, one_round(): pl.pallas_call(round_kernel, out_shape=(like(table), like(state), like(ta...  23.7 us
    unnamed x16, local copies, waits for them, and re-layouts  2.23 us

profile of v4, /device:TPU:1, one launch (start us, length us, event | category | flops | bytes accessed | tf_op | source)
XLA Modules:
  0.0 93.0 jit_solution(2514726075527009575)
XLA Ops:
  0.6 0.0 copy-start.7
  0.6 0.6 copy-done.7
  1.3 0.7 fusion
  2.0 0.0 copy-start.4
  2.7 0.0 copy-start.3
  2.7 0.0 copy-start.2
  4.7 0.0 copy-start.5
  4.7 0.0 copy-start.6
  4.7 0.0 copy-done.4
  4.7 0.0 copy-done.3
  4.7 0.0 copy-done.2
  4.7 0.6 copy-done.5
  5.3 0.0 copy-done.6
  5.4 0.0 copy-start.1
  5.4 0.9 copy-done.1
  6.3 0.4 pack.1
  6.7 24.6 %conditional.4 = ((bf16[400,512]{1,0:T(8,128)(2,1)S(1)}, bf16[400,128]{1,0:T(8,128)(2,1)S(1)}, s32[8,256]{1,0:T(8,128)S(1)})) conditional(s32[]{:T(128)} %bitcast.3, (bf16[400,128]{1,0:T(8,128)(2,1)S(1)}, s32[8,256]{1,0:T(8,128)S(1)}) %tuple.152, (bf16[400,128]{1,0:T(8,128)(2,1)S(1)}, ...), branch_computations={%region_0.0_spmd, %region_1.0_spmd, %region_2.0_spmd, %region_3.0_... | conditional | bytes 8 | solution.py:408
  6.8 24.5 %far_15.2 = (bf16[400,512]{1,0:T(8,128)(2,1)S(1)}, bf16[400,128]{1,0:T(8,128)(2,1)S(1)}, s32[8,256]{1,0:T(8,128)S(1)}) custom-call(bf16[400,128]{1,0:T(8,128)(2,1)S(1)} %get-tuple-element.222.mine, s32[8,256]{1,0:T(8,128)S(1)} %get-tuple-element.223.idx), custom_call_target="tpu_custom_call" | custom-call | tf_op jit(solution)/shard_map/cond/branch_15_fun/far_15/pallas_call | solution.py:343
  31.3 0.0 copy-start
  31.3 11.6 %conditional.5 = ((bf16[400,512]{1,0:T(8,128)(2,1)S(1)}, s32[8,256]{1,0:T(8,128)S(1)})) conditional(s32[]{:T(128)} %bitcast.2, (bf16[400,128]{1,0:T(8,128)(2,1)S(1)}, s32[8,256]{1,0:T(8,128)S(1)}) %tuple.153, (bf16[400,128]{1,0:T(8,128)(2,1)S(1)}, s32[8,256]{1,0:T(8,128)S(1)}) %tuple.153, ...), branch_computations={%region_16.0_spmd, %region_17.0_spmd, %region_18.0_spmd, %region_1... | conditional | bytes 8 | solution.py:409
  31.4 11.6 %near_7.2 = (bf16[400,512]{1,0:T(8,128)(2,1)S(1)}, s32[8,256]{1,0:T(8,128)S(1)}) custom-call(bf16[400,128]{1,0:T(8,128)(2,1)S(1)} %get-tuple-element.238.shard, s32[8,256]{1,0:T(8,128)S(1)} %get-tuple-element.239.idx), custom_call_target="tpu_custom_call" | custom-call | tf_op jit(solution)/shard_map/cond/branch_7_fun/near_7/pallas_call | solution.py:355
  43.0 0.0 copy-done
  43.0 11.9 %one_round.2 = (f32[400,128]{1,0:T(8,128)S(1)}, f32[1,128]{1,0:T(1,128)S(1)}, bf16[400,128]{1,0:T(8,128)(2,1)S(1)}) custom-call(bf16[400,512]{1,0:T(8,128)(2,1)S(1)} %get-tuple-element.318.other, s32[8,256]{1,0:T(8,128)S(1)} %get-tuple-element.319.other_idx, bf16[400,512]{1,0:T(8,128)(2,1)S(1)} %get-tuple-element.320.own, ...), custom_call_target="tpu_custom_call" | custom-call | tf_op jit(solution)/shard_map/one_round/pallas_call | solution.py:369
  54.9 13.2 %conditional.6 = ((bf16[400,512]{1,0:T(8,128)(2,1)S(1)}, bf16[400,128]{1,0:T(8,128)(2,1)S(1)}, s32[8,256]{1,0:T(8,128)S(1)})) conditional(s32[]{:T(128)} %bitcast.1, (bf16[400,128]{1,0:T(8,128)(2,1)S(1)}, s32[8,256]{1,0:T(8,128)S(1)}) %tuple.154, (bf16[400,128]{1,0:T(8,128)(2,1)S(1)}, ...), branch_computations={%region_24.0_spmd, %region_25.0_spmd, %region_26.0_spmd, %region_2... | conditional | bytes 8 | solution.py:408
  54.9 13.2 %far_6.3 = (bf16[400,512]{1,0:T(8,128)(2,1)S(1)}, bf16[400,128]{1,0:T(8,128)(2,1)S(1)}, s32[8,256]{1,0:T(8,128)S(1)}) custom-call(bf16[400,128]{1,0:T(8,128)(2,1)S(1)} %get-tuple-element.252.mine, s32[8,256]{1,0:T(8,128)S(1)} %get-tuple-element.253.idx), custom_call_target="tpu_custom_call" | custom-call | tf_op jit(solution)/shard_map/cond/branch_6_fun/far_6/pallas_call | solution.py:343
  68.1 12.4 %conditional.7 = ((bf16[400,512]{1,0:T(8,128)(2,1)S(1)}, s32[8,256]{1,0:T(8,128)S(1)})) conditional(s32[]{:T(128)} %bitcast, (bf16[400,128]{1,0:T(8,128)(2,1)S(1)}, s32[8,256]{1,0:T(8,128)S(1)}) %tuple.155, (bf16[400,128]{1,0:T(8,128)(2,1)S(1)}, s32[8,256]{1,0:T(8,128)S(1)}) %tuple.155, ...), branch_computations={%region_40.0_spmd, %region_41.0_spmd, %region_42.0_spmd, %region_4... | conditional | bytes 8 | solution.py:409
  68.3 12.1 %near_6.3 = (bf16[400,512]{1,0:T(8,128)(2,1)S(1)}, s32[8,256]{1,0:T(8,128)S(1)}) custom-call(bf16[400,128]{1,0:T(8,128)(2,1)S(1)} %get-tuple-element.284.shard, s32[8,256]{1,0:T(8,128)S(1)} %get-tuple-element.285.idx), custom_call_target="tpu_custom_call" | custom-call | tf_op jit(solution)/shard_map/cond/branch_6_fun/near_6/pallas_call | solution.py:355
  80.5 11.8 %one_round.3 = (f32[400,128]{1,0:T(8,128)S(1)}, f32[1,128]{1,0:T(1,128)S(1)}, bf16[400,128]{1,0:T(8,128)(2,1)}) custom-call(bf16[400,512]{1,0:T(8,128)(2,1)S(1)} %get-tuple-element.328.other, s32[8,256]{1,0:T(8,128)S(1)} %get-tuple-element.329.other_idx, bf16[400,512]{1,0:T(8,128)(2,1)S(1)} %get-tuple-element.330.own, ...), custom_call_target="tpu_custom_call" | custom-call | tf_op jit(solution)/shard_map/one_round/pallas_call | solution.py:369
  92.3 0.7 hand_over.1
  (1 shorter events, 0.0 us)
Async XLA Ops:
  0.6 0.7 copy-start.7
  2.0 2.8 %copy-start.4 = (s32[2,1,512]{2,1,0:T(1,128)S(1)}, s32[2,1,512]{2,1,0:T(1,128)}, u32[]{:S(2)}) copy-start(s32[2,1,512]{2,1,0:T(1,128)} %refs_3_.1) | copy-start | bytes 12292
  2.7 2.1 %copy-start.3 = (s32[2,2,1,2,256]{4,3,2,1,0:T(2,128)S(1)}, s32[2,2,1,2,256]{4,3,2,1,0:T(2,128)}, u32[]{:S(2)}) copy-start(s32[2,2,1,2,256]{4,3,2,1,0:T(2,128)} %refs_4_.1) | copy-start | bytes 24580
  2.7 2.1 %copy-start.2 = (s32[2,2,1,512]{3,2,1,0:T(1,128)S(1)}, s32[2,2,1,512]{3,2,1,0:T(1,128)}, u32[]{:S(2)}) copy-start(s32[2,2,1,512]{3,2,1,0:T(1,128)} %refs_2_.1) | copy-start | bytes 24580
  4.7 0.7 copy-start.5
  4.7 0.7 copy-start.6
  5.4 0.9 %copy-start.1 = (f32[128,400]{0,1:T(8,128)S(1)}, f32[128,400]{0,1:T(8,128)}, u32[]{:S(2)}) copy-start(f32[128,400]{0,1:T(8,128)} %param.56) | copy-start | bytes 614404
  31.3 11.7 %copy-start = (bf16[256,400]{0,1:T(8,128)(2,1)S(1)}, bf16[256,400]{0,1:T(8,128)(2,1)}, u32[]{:S(2)}) copy-start(bf16[256,400]{0,1:T(8,128)(2,1)} %param.58) | copy-start | bytes 614404
